TPU v7x, 32 devices: a whole 2x2x4 slice. The times are simulated.
32 devices in a mesh: dp: 8 (over y, x, core), tensor: 4 (over z).
Axes of the slice: x: 2, y: 2, z: 4, core: 2. Of those that a mesh axis runs over, the one named last changes fastest.
Arguments:
- inputs: bfloat16 [16384, 1280], P(('dp', 'tensor')), may hold values from -6 to 6
- cotangent: bfloat16 [16384, 1280], P(('dp', 'tensor')), may hold values from -6 to 6
- gain_attn: float32 [1280], replicated, may hold values from 0.1 to 1.9
- gain_mlp: float32 [1280], replicated, may hold values from 0.1 to 1.9
- query_scale: float32 [80], replicated, may hold values from -0.5 to 1.5
- w_query: bfloat16 [1280, 1280], P(None, 'tensor'), may hold values from -0.15625 to 0.15625
- w_key: bfloat16 [1280, 1280], P(None, 'tensor'), may hold values from -0.15625 to 0.15625
- w_value: bfloat16 [1280, 1280], P(None, 'tensor'), may hold values from -0.15625 to 0.15625
- w_out: bfloat16 [1280, 1280], P('tensor'), may hold values from -1 to 1
- w_up: bfloat16 [1280, 1280], P(None, 'tensor'), may hold values from -0.15625 to 0.15625
- w_down: bfloat16 [1280, 1280], P('tensor'), may hold values from -0.15625 to 0.15625
- lengths: int32 [8], P('dp'), may hold values from 1024 to 2048, as said below
- offsets: int32 [8], P('dp'), may hold values from 0 to 1024, as said below
Outputs:
- output: bfloat16 [16384, 1280], P(('dp', 'tensor'))
- grad_input: float32 [16384, 1280], P(('dp', 'tensor'))
- grad_gain_attn: float32 [1280], replicated
- grad_gain_mlp: float32 [1280], replicated
- grad_query_scale: float32 [80], replicated
- grad_query: float32 [1280, 1280], P(None, 'tensor')
- grad_key: float32 [1280, 1280], P(None, 'tensor')
- grad_value: float32 [1280, 1280], P(None, 'tensor')
- grad_out: float32 [1280, 1280], P('tensor')
- grad_up: float32 [1280, 1280], P(None, 'tensor')
- grad_down: float32 [1280, 1280], P('tensor')
Inputs may be any that keep to these rules, and one draw needn't show every extreme that they name: `lengths`: one group's sequence fills all 2048 slots and another's is exactly 1024 long. `offsets`: a sequence never runs past its group's 2048 slots; the group whose length is 1024 starts at 1024.
All inputs are finite; a program needn't handle non-finite values.
Results may differ from a plain program's by a relative error of at most 0.018.
Values may be sent and summed in bfloat16 or wider, within the bound.
A program may use at most 256 MiB of HBM per device.

v0:
```python
import functools
import math

import jax
import jax.numpy as jnp
from jax import lax
from jax.experimental import pallas as pl
from jax.experimental.pallas import tpu as pltpu
from jax.sharding import PartitionSpec as P

EPSILON = 1e-06
LOG_TWO_E = 1.4426950408889634
MESH_ID = pl.DeviceIdType.MESH
CHUNKS = 4


def rms_forward(values, gain):
    inverse = lax.rsqrt(jnp.mean(values * values, axis=-1, keepdims=True) + EPSILON)
    return (values * inverse * gain, inverse)


def rms_backward(values, inverse, gain, grad_normed):
    scaled = values * inverse
    grad_scaled = grad_normed * gain
    return inverse * (
        grad_scaled - scaled * jnp.mean(grad_scaled * scaled, axis=-1, keepdims=True)
    )


class Place:
    def __init__(self):
        self.d = lax.axis_index("dp")
        self.t = lax.axis_index("tensor")
        self.c = lax.rem(self.d, 2)
        self.g = self.t // 2
        self.base = self.d - self.c
        self.pairs = lax.axis_size("dp") // 2
        self.pair = self.d // 2
        self.main = self.c == self.g
        self.pos = jnp.where(self.c == 0, self.t, 3 - self.t)

    def device(self, seq, pos):
        return (self.base + seq, jnp.where(seq == 0, pos, 3 - pos))

    def across(self, step):
        return (2 * lax.rem(self.pair + step, self.pairs) + self.c, self.t)

    def partner(self):
        return (self.base + 1 - self.c, self.t)

    def quarter(self):
        return jnp.where(self.main, self.t, lax.rem(self.t + 2, 4))


def pair_barrier(here, plane=False):
    barrier = pltpu.get_barrier_semaphore()
    others = []
    for step in range(1, 8):
        code = lax.rem(here.c * 4 + here.t + step, 8)
        others.append((here.base + code // 4, lax.rem(code, 4)))
    if plane:
        others += [here.across(step) for step in range(1, here.pairs)]
    for device in others:
        pl.semaphore_signal(barrier, inc=1, device_id=device, device_id_type=MESH_ID)
    pl.semaphore_wait(barrier, len(others))


def remote(src, dst, send, recv, device):
    return pltpu.make_async_remote_copy(
        src_ref=src, dst_ref=dst, send_sem=send, recv_sem=recv, device_id=device, device_id_type=MESH_ID
    )


def dg(left, right, left_dim, right_dim):
    return lax.dot_general(
        left, right, (((left_dim,), (right_dim,)), ((), ())), preferred_element_type=jnp.float32
    )


TILE = 512
MASKED = -1e30


def readable(span, first_key, first_query):
    shape = (TILE, TILE)
    key = first_key + lax.broadcasted_iota(jnp.int32, shape, 0)
    query = first_query + lax.broadcasted_iota(jnp.int32, shape, 1)
    valid = (key >= span[1]) & (key < span[1] + span[0])
    return (valid & (key <= query)) | (key == query)


def key_bias(span, first_key):
    key = first_key + lax.broadcasted_iota(jnp.int32, (TILE, 1), 0)
    return jnp.where((key >= span[1]) & (key < span[1] + span[0]), 0.0, MASKED)


def forward_kernel(
    span, own, native, factor, mlp_native,
    gathered, weights, qkv, out, logsum, rows_out, mlp_out, mlp_up, mlp_down,
    highest, summed, total,
    keep_sem, send_z, send_c, recv,
    native_sem, weight_sent, spread_sent, weight_got,
    rows_sent, rows_got, rows_local,
    mlp_local, line_sent, line_got, plane_sent, share_sent, mlp_have,
):
    heads = logsum.shape[0]
    width, slots = out.shape
    dim = width // heads
    low, f32 = qkv.dtype, jnp.float32
    here = Place()
    pairs = here.pairs
    split = mlp_native.shape[1]
    rows = own.shape[0]
    part = rows // CHUNKS
    columns = own.shape[1] // 2
    tall = native.shape[0] // split
    blocks = slots // TILE
    partner = here.partner()
    pair_barrier(here, plane=True)

    def half(core):
        return pl.ds(pl.multiple_of(core * columns, columns), columns)

    def weight_piece(ref, pair, core):
        return ref.at[pl.ds(pl.multiple_of(pair * tall, tall), tall), half(core)]

    line = lax.rem(here.t + 2, 4)
    weight_copy = remote(
        weight_piece(native, here.pair, here.c),
        weight_piece(weights, here.pair, here.c),
        weight_sent,
        weight_got.at[here.pair, here.c],
        (here.base + 1 - line // 2, line),
    )
    sends = here.pair < split

    @pl.when(sends)
    def _():
        weight_copy.start()

    native_copy = pltpu.make_async_copy(native, weights, native_sem)

    @pl.when(here.main)
    def _():
        native_copy.start()

    def place(seq, k, ch):
        block = jnp.where(seq == 0, k, 3 - k)
        return gathered.at[pl.ds(pl.multiple_of(block * rows + ch * part, part), part)]

    def copy(src, k, ch, seq, device, send):
        return remote(src, place(seq, k, ch), send.at[k, ch], recv.at[k, ch], device)

    def own_copy(k, ch, device, send):
        return copy(own.at[pl.ds(ch * part, part)], k, ch, here.c, device, send)

    def pass_copy(k, ch, device, send):
        return copy(place(here.g, k, ch), k, ch, here.g, device, send)

    def arrived(k, ch):
        pass_copy(k, ch, partner, send_z).wait_recv()

    keep = pltpu.make_async_copy(
        own, gathered.at[pl.ds(pl.multiple_of(here.t * rows, rows), rows)], keep_sem
    )
    near = here.device(here.c, jnp.where(here.pos == 1, 0, 1))

    @pl.when(here.main)
    def _():
        keep.start()
        for ch in range(CHUNKS):
            own_copy(here.pos, ch, near, send_z).start()
            own_copy(here.pos, ch, partner, send_c).start()

    @pl.when(jnp.logical_not(here.main))
    def _():
        for ch in range(CHUNKS):
            own_copy(here.pos, ch, near, send_z).start()

    kept = (mlp_out, mlp_up, mlp_down)

    def mlp_piece(w, quarter, pair, core):
        return kept[w].at[quarter, pair, :, half(core)]

    def mlp_line(w, step):
        return remote(
            mlp_native.at[w, here.pair, :, half(here.c)],
            mlp_piece(w, here.t, here.pair, here.c),
            line_sent.at[w, step - 1],
            line_got.at[w, here.t],
            (here.d, lax.rem(here.t + step, 4)),
        )

    def mlp_plane(w, n, step):
        quarter = lax.rem(here.t + n, 4)
        piece = mlp_piece(w, quarter, here.pair, here.c)
        return remote(
            piece, piece, plane_sent.at[w, n - 1, step], mlp_have.at[w, quarter, here.pair, here.c],
            here.across(step),
        )

    def mlp_core(w, n, pair):
        quarter = lax.rem(here.t + n, 4)
        piece = mlp_piece(w, quarter, pair, here.c)
        return remote(
            piece, piece, share_sent.at[w, n - 1, pair], mlp_have.at[w, quarter, pair, here.c], partner
        )

    def mlp_arrived(w, n, pair, core):
        quarter = lax.rem(here.t + n, 4)
        piece = mlp_piece(w, quarter, pair, core)
        remote(
            piece, piece, share_sent.at[0, 0, 0], mlp_have.at[w, quarter, pair, core], partner
        ).wait_recv()

    def mlp_keep(w):
        return pltpu.make_async_copy(mlp_native.at[w], kept[w].at[here.t], mlp_local.at[w])

    def to_line(w):
        @pl.when(sends)
        def _():
            for step in range(1, 4):
                mlp_line(w, step).start()

    to_line(0)
    to_line(1)
    to_line(2)
    for w in range(3):
        mlp_keep(w).start()

    def from_line(w):
        @pl.when(sends)
        def _():
            for n in (1, 3, 2):
                quarter = lax.rem(here.t + n, 4)
                piece = mlp_piece(w, quarter, here.pair, here.c)
                remote(
                    piece, piece, share_sent.at[0, 0, 0], line_got.at[w, quarter], partner
                ).wait_recv()
                for step in range(1, pairs):
                    mlp_plane(w, n, step).start()
                mlp_core(w, n, here.pair).start()

    def spread(core, step):
        piece = weight_piece(weights, here.pair, core)
        return remote(
            piece, piece, spread_sent.at[core, step - 1], weight_got.at[here.pair, core], here.across(step)
        )

    def weight_arrived(pair, core):
        piece = weight_piece(weights, pair, core)
        remote(piece, piece, weight_sent, weight_got.at[pair, core], partner).wait_recv()

    @pl.when(jnp.logical_not(here.main))
    def _():
        @pl.when(sends)
        def _():
            for core in range(2):
                weight_arrived(here.pair, core)
                for step in range(1, pairs):
                    spread(core, step).start()

        for pair in range(split):
            @pl.when(here.pair != pair)
            def _(pair=pair):
                for core in range(2):
                    weight_arrived(pair, core)

    @pl.when(here.main)
    def _():
        native_copy.wait()
        keep.wait()

    @pl.when(here.pos == 1)
    def _():
        for ch in range(CHUNKS):
            arrived(2, ch)
            pass_copy(2, ch, near, send_z).start()
            pass_copy(2, ch, partner, send_c).start()
            arrived(0, ch)
            pass_copy(0, ch, partner, send_c).start()
        for ch in range(CHUNKS):
            arrived(3, ch)
            pass_copy(3, ch, near, send_z).start()
            pass_copy(3, ch, partner, send_c).start()

    quarter = here.quarter()

    def into(q):
        return rows_out.at[pl.ds(pl.multiple_of(q * width, width), width)]

    def done_columns(i):
        return out.at[:, pl.ds(pl.multiple_of(i * TILE, TILE), TILE)]

    def rows_copy(i):
        return remote(
            done_columns(i), into(quarter), rows_sent.at[i], rows_got.at[quarter], (here.base + here.g, i)
        )

    rows_keep = pltpu.make_async_copy(done_columns(here.t), into(here.t), rows_local)

    def finish(i):
        qs = pl.ds(pl.multiple_of(i * TILE, TILE), TILE)
        for h in range(heads):
            hs = pl.ds(h * dim, dim)
            sums = summed[h : h + 1, qs]
            out[hs, qs] = (total[hs, qs] / sums).astype(out.dtype)
            logsum[h : h + 1, qs] = highest[h : h + 1, qs] + jnp.log(sums)
        stays = here.main & (here.t == i)

        @pl.when(stays)
        def _():
            rows_keep.start()

        @pl.when(jnp.logical_not(stays))
        def _():
            rows_copy(i).start()

    highest[...] = jnp.full_like(highest, MASKED)
    summed[...] = jnp.zeros_like(summed)
    total[...] = jnp.zeros_like(total)

    @pl.loop(0, blocks)
    def _(s):
        b = jnp.where(here.g == 0, s, blocks - 1 - s)
        last = (here.g == 1) & (s == blocks - 1)

        @pl.when((here.pos == 0) & (s >= 1))
        def _():
            for ch in range(CHUNKS):
                arrived(s, ch)
                pass_copy(s, ch, partner, send_c).start()

        @pl.when(jnp.logical_not(here.main))
        def _():
            for ch in range(CHUNKS):
                arrived(s, ch)

        @pl.when(s == 0)
        def _():
            from_line(0)

        @pl.when(s == 1)
        def _():
            from_line(1)

        @pl.when(s == 2)
        def _():
            from_line(2)

        bs = pl.ds(pl.multiple_of(b * TILE, TILE), TILE)
        for w in range(3):
            at = pl.ds(w * width, width)
            qkv[at, bs] = (dg(weights[at], gathered[bs], 1, 1) * factor[at]).astype(low)

        def tile(i, j, diagonal):
            qs = pl.ds(pl.multiple_of(i * TILE, TILE), TILE)
            ks = pl.ds(pl.multiple_of(j * TILE, TILE), TILE)
            if diagonal:
                allowed = readable(span, j * TILE, i * TILE)
            else:
                bias = key_bias(span, j * TILE)
            for h in range(heads):
                hs = pl.ds(h * dim, dim)
                scores = dg(qkv[pl.ds(width + h * dim, dim), ks], qkv[hs, qs], 0, 0)
                scores = jnp.where(allowed, scores, MASKED) if diagonal else scores + bias
                before = highest[h : h + 1, qs]
                after = jnp.maximum(before, jnp.max(scores, axis=0, keepdims=True))
                expo = jnp.exp(scores - after)
                scale = jnp.exp(before - after)
                summed[h : h + 1, qs] = summed[h : h + 1, qs] * scale + jnp.sum(expo, axis=0, keepdims=True)
                highest[h : h + 1, qs] = after
                total[hs, qs] = total[hs, qs] * scale + dg(
                    qkv[pl.ds(2 * width + h * dim, dim), ks], expo.astype(low), 1, 0
                )

        tile(b, b, True)

        @pl.when(last)
        def _():
            finish(b)

        @pl.loop(0, s)
        def _(n):
            i = jnp.where(here.g == 0, b, b + 1 + n)
            tile(i, jnp.where(here.g == 0, n, b), False)

            @pl.when(last)
            def _():
                finish(i)

        @pl.when(here.g == 0)
        def _():
            finish(b)


    for w in range(3):
        for n in (1, 3, 2):
            for pair in range(split):
                @pl.when(here.pair != pair)
                def _(w=w, n=n, pair=pair):
                    mlp_arrived(w, n, pair, here.c)
                    mlp_core(w, n, pair).start()

    for block in range(4):
        stays = here.main & (here.t == block)

        @pl.when(stays)
        def _():
            rows_keep.wait()

        @pl.when(jnp.logical_not(stays))
        def _(block=block):
            rows_copy(block).wait_send()
            remote(
                done_columns(0), into(block), rows_sent.at[0], rows_got.at[block], partner
            ).wait_recv()

    for w in range(3):
        for n in range(1, 4):
            for pair in range(split):
                mlp_arrived(w, n, pair, 1 - here.c)
                mlp_core(w, n, pair).wait_send()
        mlp_keep(w).wait()

    @pl.when(sends)
    def _():
        weight_copy.wait_send()
        for w in range(3):
            for step in range(1, 4):
                mlp_line(w, step).wait_send()
                for across in range(1, pairs):
                    mlp_plane(w, step, across).wait_send()

    @pl.when(sends & jnp.logical_not(here.main))
    def _():
        for core in range(2):
            for step in range(1, pairs):
                spread(core, step).wait_send()

    for ch in range(CHUNKS):
        own_copy(here.pos, ch, near, send_z).wait_send()

    @pl.when(here.main)
    def _():
        for ch in range(CHUNKS):
            own_copy(here.pos, ch, partner, send_c).wait_send()

    @pl.when(here.pos == 0)
    def _():
        for k in (1, 2, 3):
            for ch in range(CHUNKS):
                pass_copy(k, ch, partner, send_c).wait_send()

    @pl.when(here.pos == 1)
    def _():
        for ch in range(CHUNKS):
            pass_copy(0, ch, partner, send_c).wait_send()
            for k in (2, 3):
                pass_copy(k, ch, near, send_z).wait_send()
                pass_copy(k, ch, partner, send_c).wait_send()


def attention_forward(span, own, native, factor, mlp_native, heads):
    rows, model = own.shape
    slots = 4 * rows
    width = native.shape[0] // 3
    _, split, tall, _ = mlp_native.shape
    pairs = lax.axis_size("dp") // 2
    low, f32 = own.dtype, jnp.float32
    vmem = pl.BlockSpec(memory_space=pltpu.VMEM)
    hbm = pl.BlockSpec(memory_space=pl.ANY)
    dma = pltpu.SemaphoreType.DMA
    return pl.pallas_call(
        forward_kernel,
        out_shape=(
            jax.ShapeDtypeStruct((slots, model), low),
            jax.ShapeDtypeStruct(native.shape, low),
            jax.ShapeDtypeStruct((3 * width, slots), low),
            jax.ShapeDtypeStruct((width, slots), low),
            jax.ShapeDtypeStruct((heads, slots), f32),
            jax.ShapeDtypeStruct((4 * width, rows), low),
        )
        + (jax.ShapeDtypeStruct((4, split, tall, model), low),) * 3,
        in_specs=[pl.BlockSpec(memory_space=pltpu.SMEM), hbm, hbm, vmem, hbm],
        out_specs=(vmem,) * 5 + (hbm,) * 4,
        scratch_shapes=[
            pltpu.VMEM((heads, slots), f32),
            pltpu.VMEM((heads, slots), f32),
            pltpu.VMEM((width, slots), f32),
            dma,
            dma((4, CHUNKS)),
            dma((4, CHUNKS)),
            dma((4, CHUNKS)),
            dma,
            dma,
            dma((2, pairs - 1)),
            dma((split, 2)),
            dma((4,)),
            dma((4,)),
            dma,
            dma((3,)),
            dma((3, 3)),
            dma((3, 4)),
            dma((3, 3, pairs)),
            dma((3, 3, split)),
            dma((3, 4, split, 2)),
        ],
        compiler_params=pltpu.CompilerParams(
            collective_id=1, has_side_effects=True, vmem_limit_bytes=50 * 1024 * 1024
        ),
        name="attention_forward",
    )(span, own, native, factor, mlp_native)


def middle_kernel(
    span, gain, attended, residual, cotangent, w_out_in, w_up_in, w_down_in,
    output, grad_hidden, chip_sum, small, grad,
    w_out, w_up, w_down, second, activated, grad_low, grad_pre, branch, grad_att, weight_grad,
    load_sem, split_sent, split_got, local_sem, give_sent, give_got,
):
    here = Place()
    low, f32 = output.dtype, jnp.float32
    rows, model = output.shape
    width = grad.shape[0]
    pairs, tall = weight_grad.shape[2], weight_grad.shape[3]
    half_rows = rows // 2
    partner = here.partner()
    loads = [
        pltpu.make_async_copy(src, dst, load_sem.at[w])
        for w, (src, dst) in enumerate(((w_out_in, w_out), (w_up_in, w_up), (w_down_in, w_down)))
    ]
    for load in loads:
        load.start()
    pair_barrier(here)

    def of(q, r):
        return grad_att.at[
            pl.ds(pl.multiple_of(q * width, width), width), pl.ds(pl.multiple_of(r * half_rows, half_rows), half_rows)
        ]

    def into(block, r):
        return grad.at[:, pl.ds(pl.multiple_of(block * rows + r * half_rows, half_rows), half_rows)]

    def split_copy(q, r):
        native = (q // 2) == here.c
        seq = jnp.where(native, here.c, 1 - here.c)
        line = jnp.where(native, q, (q + 2) % 4)
        return remote(
            of(q, r), into(here.t, r), split_sent.at[q, r], split_got.at[here.t, r], (here.base + seq, line)
        )

    def keep(r):
        return pltpu.make_async_copy(of(here.t, r), into(here.t, r), local_sem.at[r])

    loads[0].wait()

    @pl.loop(0, 2)
    def _(r):
        at = pl.ds(pl.multiple_of(r * half_rows, half_rows), half_rows)
        hidden = residual[at].astype(f32) + dg(attended[:, at], w_out[...], 0, 0)
        inverse = lax.rsqrt(jnp.mean(hidden * hidden, axis=-1, keepdims=True) + EPSILON)
        scaled = hidden * inverse
        second[at] = (scaled * gain[...]).astype(low)

        @pl.when(r == 0)
        def _():
            loads[1].wait()

        before = dg(second[at], w_up[...], 1, 1)
        sigmoid = jax.nn.sigmoid(before)
        activated[at] = (before * sigmoid).astype(low)

        @pl.when(r == 0)
        def _():
            loads[2].wait()

        position = here.t * rows + r * half_rows + lax.broadcasted_iota(jnp.int32, (half_rows, 1), 0)
        valid = (position >= span[1]) & (position < span[1] + span[0])
        grad_out = jnp.where(valid, cotangent[at].astype(f32), 0.0)
        grad_low[at] = grad_out.astype(low)
        grad_act = dg(grad_low[at], w_down[...], 1, 1)
        grad_pre[at] = (grad_act * (sigmoid * (1.0 + before * (1.0 - sigmoid)))).astype(low)
        grad_scaled = dg(grad_pre[at], w_up[...], 1, 0) * gain[...]
        grad_rows = grad_out + inverse * (
            grad_scaled - scaled * jnp.mean(grad_scaled * scaled, axis=-1, keepdims=True)
        )
        grad_hidden[at] = grad_rows
        branch[at] = grad_rows.astype(low)
        grad_att[:, at] = dg(w_out[...], branch[at], 1, 1).astype(low)
        for q in range(4):
            stays = here.main & (here.t == q)

            @pl.when(stays)
            def _():
                keep(r).start()

            @pl.when(jnp.logical_not(stays))
            def _(q=q):
                split_copy(q, r).start()

        output[at] = (hidden + dg(activated[at], w_down[...], 1, 0)).astype(low)

    columns = chip_sum.shape[-1]
    two = 2 * width

    def half(core):
        return pl.ds(pl.multiple_of(core * columns, columns), columns)

    def give(w):
        return remote(
            weight_grad.at[w, :, :, :, half(1 - here.c)], chip_sum.at[w], give_sent.at[w], give_got.at[w], partner
        )

    small[...] = jnp.zeros_like(small)
    for w in range(3):
        for quarters in range(2):
            at = pl.ds(quarters * two, two)
            if w == 0:
                grads = dg(attended[at], branch[...], 1, 0)
            elif w == 1:
                grads = dg(grad_pre[:, at], second[...], 0, 0)
                small[1:2] += jnp.sum(grads * w_up[at].astype(f32), axis=0, keepdims=True)
            else:
                grads = dg(activated[:, at], grad_low[...], 0, 0)
            for q in range(2):
                for p in range(pairs):
                    first = q * width + p * tall
                    weight_grad[w, 2 * quarters + q, p] = grads[first : first + tall].astype(low)
        give(w).start()

    for w in range(3):
        give(w).wait_recv()

        @pl.loop(0, 4)
        def _(q, w=w):
            @pl.loop(0, pairs)
            def _(p):
                mine = weight_grad[w, q, p, :, half(here.c)]
                chip_sum[w, q, p] = (chip_sum[w, q, p].astype(f32) + mine.astype(f32)).astype(low)

    for r in range(2):
        for q in range(4):
            stays = here.main & (here.t == q)

            @pl.when(stays)
            def _(r=r):
                keep(r).wait()

            @pl.when(jnp.logical_not(stays))
            def _(q=q, r=r):
                remote(of(0, r), into(q, r), split_sent.at[0, r], split_got.at[q, r], partner).wait_recv()
                split_copy(q, r).wait_send()

    for w in range(3):
        give(w).wait_send()


def feed_forward(span, gain, attended, residual, cotangent, w_out, w_up, w_down, width, pairs):
    rows, model = residual.shape
    low, f32 = residual.dtype, jnp.float32
    vmem = pl.BlockSpec(memory_space=pltpu.VMEM)
    hbm = pl.BlockSpec(memory_space=pl.ANY)
    dma = pltpu.SemaphoreType.DMA
    tall = width // pairs
    return pl.pallas_call(
        middle_kernel,
        out_shape=(
            jax.ShapeDtypeStruct((rows, model), low),
            jax.ShapeDtypeStruct((rows, model), f32),
            jax.ShapeDtypeStruct((3, 4, pairs, tall, model // 2), low),
            jax.ShapeDtypeStruct((8, model), f32),
            jax.ShapeDtypeStruct((width, 4 * rows), low),
        ),
        in_specs=[pl.BlockSpec(memory_space=pltpu.SMEM)] + [vmem] * 4 + [hbm] * 3,
        out_specs=(vmem,) * 4 + (hbm,),
        scratch_shapes=[pltpu.VMEM((model, model), low)] * 3
        + [pltpu.VMEM((rows, model), low)] * 5
        + [
            pltpu.VMEM((model, rows), low),
            pltpu.VMEM((3, 4, pairs, tall, model), low),
            dma((3,)),
            dma((4, 2)),
            dma((4, 2)),
            dma((2,)),
            dma((3,)),
            dma((3,)),
        ],
        compiler_params=pltpu.CompilerParams(
            collective_id=3, has_side_effects=True, vmem_limit_bytes=65_000_000
        ),
        name="feed_forward",
    )(span, gain, attended, residual, cotangent, w_out, w_up, w_down)


def backward_kernel(
    span, qkv, out, logsum, factor, weights, small, grad, chip_sum, gathered,
    rows_grad, out_final, up_final, down_final, qkv_all, small_all,
    result, query_sum, key_sum, value_sum, term,
    partial, from_core, from_line, own_sum, pass_sum, plane_in,
    normed, scale_sum, weight_grad, qkv_in, qkv_swap, mlp_in, mlp_sum,
    small_own, small_pair, small_plane, small_line,
    own_sem, pass_sem, plane_sent, plane_got,
    send_c, send_z, recv_c, recv_z,
    out_sem, normed_sem, qkv_sent, qkv_got, cross_sent, cross_got, qkv_spread, qkv_share, qkv_have, qkv_local,
    line_sent, line_got, mlp_spread, mlp_share, mlp_have, mlp_local,
    small_sems, small_across_sent, small_across_got, small_along_sent, small_along_got,
):
    heads = logsum.shape[0]
    width, slots = out.shape
    dim = width // heads
    low, f32 = qkv.dtype, jnp.float32
    here = Place()
    pairs = here.pairs
    rows = rows_grad.shape[0]
    part = rows // CHUNKS
    partner = here.partner()
    pair_barrier(here, plane=True)
    blocks = slots // TILE

    columns = chip_sum.shape[-1]

    def half(core):
        return pl.ds(pl.multiple_of(core * columns, columns), columns)

    square = pairs == 4
    by_x = here.pair + 1 - 2 * lax.rem(here.pair, 2)
    by_y = lax.rem(here.pair + 2, 4)
    corner = 3 - here.pair

    def at_pair(pair):
        return (2 * pair + here.c, here.t)

    def plane_first(w, side, kind):
        to, pair = (by_x, by_y)[side], ((by_x, by_y)[side], corner)[kind]
        return remote(
            chip_sum.at[w, pl.ds(2 * side, 2), pair], plane_in.at[w, side, kind],
            plane_sent.at[w, 2 * side + kind], plane_got.at[w, 2 * side + kind], at_pair(to),
        )

    def plane_second(w, side):
        return remote(
            pass_sum.at[w, side], plane_in.at[w, side, 2], plane_sent.at[w, 4 + side], plane_got.at[w, 4 + side],
            at_pair((by_y, by_x)[side]),
        )

    def plane_copy(w, step):
        return remote(
            chip_sum.at[w, :, lax.rem(here.pair + step, pairs)],
            plane_in.at[step - 1, w],
            plane_sent.at[w, step - 1],
            plane_got.at[w, step - 1],
            here.across(step),
        )

    def plane_start(w):
        if square:
            for kind in (1, 0):
                for side in range(2):
                    plane_first(w, side, kind).start()
        else:
            for step in range(1, pairs):
                plane_copy(w, step).start()

    def plane_pass(w):
        if square:
            for side in range(2):
                plane_first(w, side, 1).wait_recv()
                for q in range(2):
                    pass_sum[w, side, q] = (
                        pass_sum[w, side, q].astype(f32) + plane_in[w, side, 1, q].astype(f32)
                    ).astype(low)
                plane_second(w, side).start()

    def plane_sent_all(w):
        if square:
            for side in range(2):
                plane_first(w, side, 0).wait_send()
                plane_first(w, side, 1).wait_send()
                plane_second(w, side).wait_send()
        else:
            for step in range(1, pairs):
                plane_copy(w, step).wait_send()

    pass_loads = []
    if square:
        pass_loads = [
            pltpu.make_async_copy(
                chip_sum.at[:, pl.ds(2 * side, 2), (by_y, by_x)[side]], pass_sum.at[:, side], pass_sem.at[side]
            )
            for side in range(2)
        ]
    for load in pass_loads:
        load.start()
    own_load = pltpu.make_async_copy(chip_sum.at[:, :, here.pair], own_sum, own_sem)
    own_load.start()
    for w in range(3):
        plane_start(w)
    out_copy = pltpu.make_async_copy(out, result.at[pl.ds(0, width)], out_sem)
    out_copy.start()
    query_sum[...] = jnp.zeros_like(query_sum)
    key_sum[...] = jnp.zeros_like(key_sum)
    value_sum[...] = jnp.zeros_like(value_sum)
    out_copy.wait()
    own_load.wait()
    for load in pass_loads:
        load.wait()
    for h in range(heads):
        hs = pl.ds(h * dim, dim)
        term[h : h + 1] = jnp.sum(grad[hs].astype(f32) * result[hs].astype(f32), axis=0, keepdims=True)

    def span_of(seq, k, ch):
        block = jnp.where(seq == 0, k, 3 - k)
        return pl.ds(pl.multiple_of(block * rows + ch * part, part), part)

    def piece(k, ch):
        return pl.ds(pl.multiple_of(k * rows + ch * part, part), part)

    def line_piece(k, ch):
        return piece(k % 3 if isinstance(k, int) else lax.rem(k, 3), ch)

    def line_rows(ch):
        return pl.ds(ch * part, part)

    def core_copy(k, ch):
        at = span_of(here.g, k, ch)
        return remote(partial.at[at], from_core.at[piece(k, ch)], send_c.at[k, ch], recv_c.at[k, ch], partner)

    def line_copy(k, ch):
        at = span_of(here.g, k, ch)
        return remote(
            partial.at[at],
            from_line.at[line_piece(k, ch)],
            send_z.at[k, ch],
            recv_z.at[k, ch],
            here.device(here.c, jnp.where(here.pos == 0, 1, 0)),
        )

    def home_copy(k, ch):
        at = span_of(here.g, k, ch)
        return remote(
            partial.at[at], rows_grad.at[line_rows(ch)], send_z.at[k, ch], recv_z.at[k, ch], here.device(here.c, k)
        )

    def core_sum(k, ch):
        core_copy(k, ch).wait_recv()
        return partial[span_of(here.g, k, ch)].astype(f32) + from_core[piece(k, ch)].astype(f32)

    def with_line(k, ch):
        line_copy(k, ch).wait_recv()
        return core_sum(k, ch) + from_line[line_piece(k, ch)].astype(f32)

    def pass_on(k):
        for ch in range(CHUNKS):
            partial[span_of(here.g, k, ch)] = core_sum(k, ch).astype(low)
            line_copy(k, ch).start()

    def send_home(k):
        for ch in range(CHUNKS):
            partial[span_of(here.g, k, ch)] = with_line(k, ch).astype(low)
            home_copy(k, ch).start()

    def mlp_line(w, step):
        line = lax.rem(here.t + step, 4)
        return remote(
            own_sum.at[w, line], mlp_in.at[w, step - 1], line_sent.at[w, step - 1],
            line_got.at[w, step - 1], (here.d, line),
        )

    def plane_total(w):
        if square:
            for side in range(2):
                plane_first(w, side, 0).wait_recv()
                plane_second(w, side).wait_recv()
                for q in range(2):
                    own_sum[w, 2 * side + q] = (
                        own_sum[w, 2 * side + q].astype(f32)
                        + plane_in[w, side, 0, q].astype(f32)
                        + plane_in[w, side, 2, q].astype(f32)
                    ).astype(low)
        else:
            for step in range(1, pairs):
                plane_copy(w, step).wait_recv()

            @pl.loop(0, 4)
            def _(q):
                total = own_sum[w, q].astype(f32)
                for step in range(1, pairs):
                    total += plane_in[step - 1, w, q].astype(f32)
                own_sum[w, q] = total.astype(low)

        for step in range(1, 4):
            mlp_line(w, step).start()

    @pl.loop(0, blocks)
    def _(s):
        b = jnp.where(here.g == 0, blocks - 1 - s, s)
        k = blocks - 1 - s

        def tile(i, j, diagonal):
            qs = pl.ds(pl.multiple_of(i * TILE, TILE), TILE)
            ks = pl.ds(pl.multiple_of(j * TILE, TILE), TILE)
            if diagonal:
                allowed = readable(span, j * TILE, i * TILE)
            else:
                bias = key_bias(span, j * TILE)
            for h in range(heads):
                hs = pl.ds(h * dim, dim)
                ke = pl.ds(width + h * dim, dim)
                va = pl.ds(2 * width + h * dim, dim)
                scores = dg(qkv[ke, ks], qkv[hs, qs], 0, 0)
                scores = jnp.where(allowed, scores, MASKED) if diagonal else scores + bias
                probs = jnp.exp(scores - logsum[h : h + 1, qs])
                grad_probs = dg(qkv[va, ks], grad[hs, qs], 0, 0)
                grad_scores = (probs * (grad_probs - term[h : h + 1, qs])).astype(low)
                value_sum[hs, ks] += dg(grad[hs, qs], probs.astype(low), 1, 1)
                key_sum[hs, ks] += dg(qkv[hs, qs], grad_scores, 1, 1)
                query_sum[hs, qs] += dg(qkv[ke, ks], grad_scores, 1, 0)

        tile(b, b, True)

        @pl.when((here.pos == 0) & (s >= 1))
        def _():
            pass_on(k + 1)

        @pl.when(s >= 1)
        def _():
            plane_pass(s - 1)

        @pl.when(s >= 2)
        def _():
            plane_total(s - 2)

        @pl.loop(0, blocks - 1 - s)
        def _(n):
            tile(jnp.where(here.g == 0, b, b + 1 + n), jnp.where(here.g == 0, n, b), False)

        bs = pl.ds(pl.multiple_of(b * TILE, TILE), TILE)
        result[pl.ds(0, width), bs] = (query_sum[:, bs] * factor[...]).astype(low)
        result[pl.ds(width, width), bs] = key_sum[:, bs].astype(low)
        result[pl.ds(2 * width, width), bs] = value_sum[:, bs].astype(low)
        partial[bs] = dg(result[:, bs], weights[...], 0, 0).astype(low)

        @pl.when(jnp.logical_not(here.main))
        def _():
            for ch in range(CHUNKS):
                core_copy(k, ch).start()

    plane_total(2)

    @pl.when(here.pos == 1)
    def _():
        send_home(3)

    chunks, _, share, depth = weight_grad.shape

    half_slots = slots // 2

    def load(i, part_of):
        return pltpu.make_async_copy(
            gathered.at[
                pl.ds(part_of * half_slots, half_slots), pl.ds(pl.multiple_of(i * depth, depth), depth)
            ],
            normed.at[part_of],
            normed_sem.at[part_of],
        )

    def turn(i):
        even = lax.rem(i, 2) == 0
        return jnp.where(even, by_x, by_y), jnp.where(even, by_y, by_x)

    def qkv_send(i, step):
        if square:
            first, second = turn(i)
            to = (first, first, second)[step - 1]
            pair = (first, corner, second)[step - 1]
            device = at_pair(to)
        else:
            pair, device = lax.rem(here.pair + step, pairs), here.across(step)
        return remote(
            weight_grad.at[i, pair], qkv_in.at[i, step - 1], qkv_sent.at[i, step - 1], qkv_got.at[i, step - 1], device
        )

    first_steps = (2, 1) if square else range(1, pairs)

    small_own[...] = small[...]
    scale_sum[...] = jnp.zeros_like(scale_sum)
    load(0, 0).start()
    load(0, 1).start()

    @pl.loop(0, chunks)
    def _(i):
        at = pl.ds(pl.multiple_of(i * depth, depth), depth)
        load(i, 0).wait()
        grads = dg(result[:, :half_slots], normed[0], 1, 0)

        @pl.when(i + 1 < chunks)
        def _():
            load(i + 1, 0).start()

        load(i, 1).wait()
        grads += dg(result[:, half_slots:], normed[1], 1, 0)

        @pl.when(i + 1 < chunks)
        def _():
            load(i + 1, 1).start()

        for p in range(pairs):
            weight_grad[i, p] = grads[p * share : (p + 1) * share].astype(low)
        for step in first_steps:
            qkv_send(i, step).start()
        weighted = grads * weights[:, at].astype(f32)
        small_own[0:1, at] = jnp.sum(weighted, axis=0, keepdims=True)
        scale_sum[pl.ds(0, width)] += jnp.broadcast_to(
            jnp.sum(weighted[:width], axis=1, keepdims=True), (width, 128)
        )

    padded = scale_sum.shape[0]
    small_own[2:3, pl.ds(0, padded)] = jnp.transpose(scale_sum[...])[0:1]
    small_copy = remote(small_own, small_pair, small_sems.at[0], small_sems.at[1], partner)
    small_copy.start()

    @pl.when(here.pos == 1)
    def _():
        pass_on(0)

    def mlp_piece(w, pair, core):
        return (out_final, up_final, down_final)[w].at[pair, :, half(core)]

    def mlp_out(w, step):
        return remote(
            mlp_sum.at[w], mlp_piece(w, here.pair, here.c), mlp_spread.at[w, step], mlp_have.at[w, here.d],
            here.across(step),
        )

    def mlp_own(w):
        return remote(
            mlp_sum.at[w], mlp_piece(w, here.pair, here.c), mlp_share.at[w, 0], mlp_have.at[w, here.d], partner
        )

    def mlp_keep(w):
        return pltpu.make_async_copy(mlp_sum.at[w], mlp_piece(w, here.pair, here.c), mlp_local.at[w])

    def mlp_core(w, step):
        pair = lax.rem(here.pair + step, pairs)
        piece = mlp_piece(w, pair, here.c)
        return remote(piece, piece, mlp_share.at[w, step], mlp_have.at[w, 2 * pair + here.c], partner)

    def mlp_arrived(w, pair, core):
        remote(
            mlp_sum.at[w], mlp_piece(w, pair, core), mlp_share.at[w, 0], mlp_have.at[w, 2 * pair + core], partner
        ).wait_recv()

    @pl.when(here.pos == 1)
    def _():
        send_home(2)

    line = lax.rem(here.t + 2, 4)

    def cross(i):
        return remote(
            qkv_swap.at[0, i], qkv_swap.at[1, i], cross_sent.at[i], cross_got.at[i],
            (here.base + line // 2, line),
        )

    def qkv_piece(i, pair):
        return qkv_all.at[pair, :, pl.ds(pl.multiple_of(i * depth, depth), depth)]

    def qkv_out(i, step):
        return remote(
            qkv_swap.at[0, i], qkv_piece(i, here.pair), qkv_spread.at[i, step], qkv_have.at[i, here.pair],
            here.across(step),
        )

    def qkv_own(i):
        return remote(
            qkv_swap.at[0, i], qkv_piece(i, here.pair), qkv_share.at[i, 0], qkv_have.at[i, here.pair], partner
        )

    def qkv_keep(i):
        return pltpu.make_async_copy(qkv_swap.at[0, i], qkv_piece(i, here.pair), qkv_local.at[i])

    def qkv_core(i, step):
        pair = lax.rem(here.pair + step, pairs)
        return remote(
            qkv_piece(i, pair), qkv_piece(i, pair), qkv_share.at[i, step], qkv_have.at[i, pair], partner
        )

    def finish(i):
        @pl.when(here.main)
        def _():
            cross(i).wait_recv()
            qkv_swap[0, i] = (qkv_swap[0, i].astype(f32) + qkv_swap[1, i].astype(f32)).astype(low)
            qkv_keep(i).start()
            for step in range(1, pairs):
                qkv_out(i, step).start()
            qkv_own(i).start()

    def qkv_pass(i):
        if square:
            qkv_send(i, 2).wait_recv()
            _, second = turn(i)
            weight_grad[i, second] = (weight_grad[i, second].astype(f32) + qkv_in[i, 1].astype(f32)).astype(low)
            qkv_send(i, 3).start()

    def qkv_total(i):
        total = weight_grad[i, here.pair].astype(f32)
        for step in (1, 3) if square else range(1, pairs):
            qkv_send(i, step).wait_recv()
            total += qkv_in[i, step - 1].astype(f32)
        qkv_swap[0, i] = total.astype(low)

        @pl.when(jnp.logical_not(here.main))
        def _():
            cross(i).start()

    @pl.loop(0, chunks + 2)
    def _(n):
        @pl.when(n < chunks)
        def _():
            qkv_pass(n)

        @pl.when((n >= 1) & (n <= chunks))
        def _():
            qkv_total(n - 1)

        @pl.when(n >= 2)
        def _():
            finish(n - 2)

    for w in range(3):
        total = own_sum[w, here.t].astype(f32)
        for step in range(1, 4):
            mlp_line(w, step).wait_recv()
            total += mlp_in[w, step - 1].astype(f32)
        mlp_sum[w] = total.astype(low)
        for step in range(1, pairs):
            mlp_out(w, step).start()
        mlp_own(w).start()
        mlp_keep(w).start()

    small_copy.wait_recv()
    small_plane[here.pair] = small_own[...] + small_pair[...]

    def small_across(step):
        return remote(
            small_plane.at[here.pair], small_plane.at[here.pair], small_across_sent.at[step],
            small_across_got.at[here.pair], here.across(step),
        )

    def small_along(step):
        return remote(
            small_line.at[here.t], small_line.at[here.t], small_along_sent.at[step], small_along_got.at[here.t],
            (here.d, lax.rem(here.t + step, 4)),
        )

    for step in range(1, pairs):
        small_across(step).start()

    for step in range(1, pairs):
        pair = lax.rem(here.pair + step, pairs)
        remote(
            small_own, small_plane.at[pair], small_across_sent.at[0], small_across_got.at[pair], partner
        ).wait_recv()
    plane_total = small_plane[0]
    for pair in range(1, pairs):
        plane_total += small_plane[pair]
    small_line[here.t] = plane_total
    for step in range(1, 4):
        small_along(step).start()

    @pl.when(here.pos == 0)
    def _():
        for ch in range(CHUNKS):
            rows_grad[line_rows(ch)] = with_line(0, ch).astype(low)
        for k in (1, 2, 3):
            for ch in range(CHUNKS):
                line_copy(k, ch).wait_send()

    @pl.when(here.pos == 1)
    def _():
        for ch in range(CHUNKS):
            rows_grad[line_rows(ch)] = with_line(1, ch).astype(low)
        for ch in range(CHUNKS):
            line_copy(0, ch).wait_send()
            for k in (2, 3):
                home_copy(k, ch).wait_send()

    for k in (2, 3):
        @pl.when(here.pos == k)
        def _(k=k):
            for ch in range(CHUNKS):
                remote(
                    partial.at[piece(0, ch)], rows_grad.at[line_rows(ch)], send_z.at[0, ch], recv_z.at[k, ch], partner
                ).wait_recv()

    for step in range(1, 4):
        other = lax.rem(here.t + step, 4)
        remote(
            small_own, small_line.at[other], small_along_sent.at[0], small_along_got.at[other], partner
        ).wait_recv()
    small_all[...] = (small_line[0] + small_line[1]) + (small_line[2] + small_line[3])

    @pl.when(here.main)
    def _():
        @pl.loop(0, chunks)
        def _(i):
            for step in range(1, pairs):
                qkv_core(i, step).wait_recv()
                qkv_core(i, step).start()

    for w in range(3):
        for step in range(1, pairs):
            mlp_arrived(w, lax.rem(here.pair + step, pairs), here.c)
            mlp_core(w, step).start()

    @pl.when(here.main)
    def _():
        @pl.loop(0, chunks)
        def _(i):
            qkv_keep(i).wait()
            qkv_own(i).wait_send()
            for step in range(1, pairs):
                qkv_out(i, step).wait_send()
                qkv_core(i, step).wait_send()

    @pl.when(jnp.logical_not(here.main))
    def _():
        @pl.loop(0, chunks)
        def _(i):
            cross(i).wait_send()
            for step in range(pairs):
                qkv_core(i, step).wait_recv()

        for k in range(4):
            for ch in range(CHUNKS):
                core_copy(k, ch).wait_send()

    for w in range(3):
        for step in range(pairs):
            mlp_arrived(w, lax.rem(here.pair + step, pairs), 1 - here.c)
        mlp_keep(w).wait()
        mlp_own(w).wait_send()
        for step in range(1, pairs):
            mlp_out(w, step).wait_send()
            mlp_core(w, step).wait_send()
        for step in range(1, 4):
            mlp_line(w, step).wait_send()

    for w in range(3):
        plane_sent_all(w)

    @pl.loop(0, chunks)
    def _(i):
        for step in range(1, pairs):
            qkv_send(i, step).wait_send()

    for step in range(1, pairs):
        small_across(step).wait_send()
    for step in range(1, 4):
        small_along(step).wait_send()
    small_copy.wait_send()


DEPTH = 256


def attention_backward(
    span, qkv, out, logsum, factor, weights, small, grad, chip_sum, gathered
):
    width, slots = out.shape
    heads = logsum.shape[0]
    rows, model = slots // 4, weights.shape[1]
    low, f32 = qkv.dtype, jnp.float32
    _, _, pairs, slice_rows, columns = chip_sum.shape
    chunks, share = model // DEPTH, 3 * width // pairs
    vmem = pl.BlockSpec(memory_space=pltpu.VMEM)
    hbm = pl.BlockSpec(memory_space=pl.ANY)
    dma = pltpu.SemaphoreType.DMA
    buffer = pltpu.VMEM
    return pl.pallas_call(
        backward_kernel,
        out_shape=(
            jax.ShapeDtypeStruct((rows, model), low),
            jax.ShapeDtypeStruct((pairs, slice_rows, model), low),
            jax.ShapeDtypeStruct((pairs, slice_rows, model), low),
            jax.ShapeDtypeStruct((pairs, slice_rows, model), low),
            jax.ShapeDtypeStruct((pairs, share, model), low),
            jax.ShapeDtypeStruct(small.shape, f32),
        ),
        in_specs=[pl.BlockSpec(memory_space=pltpu.SMEM), vmem, hbm] + [vmem] * 5 + [hbm] * 2,
        out_specs=(vmem, hbm, hbm, hbm, hbm, vmem),
        scratch_shapes=[
            buffer(qkv.shape, low),
            buffer((width, slots), f32),
            buffer((width, slots), f32),
            buffer((width, slots), f32),
            buffer((heads, slots), f32),
            buffer((slots, model), low),
            buffer((slots, model), low),
            buffer((3 * rows, model), low),
            buffer((3, 4, slice_rows, columns), low),
            buffer((3, 2, 2, slice_rows, columns) if pairs == 4 else (8, 128), low),
            buffer(
                (3, 2, 3, 2, slice_rows, columns) if pairs == 4 else (pairs - 1, 3, 4, slice_rows, columns), low
            ),
            buffer((2, slots // 2, DEPTH), low),
            buffer((width + -width % 128, 128), f32),
            buffer((chunks, pairs, share, DEPTH), low),
            buffer((chunks, pairs - 1, share, DEPTH), low),
            buffer((2, chunks, share, DEPTH), low),
            buffer((3, 3, slice_rows, columns), low),
            buffer((3, slice_rows, columns), low),
            buffer(small.shape, f32),
            buffer(small.shape, f32),
            buffer((pairs,) + small.shape, f32),
            buffer((4,) + small.shape, f32),
            dma,
            dma((2,)),
            dma((3, max(6, pairs - 1))),
            dma((3, max(6, pairs - 1))),
            dma((4, CHUNKS)),
            dma((4, CHUNKS)),
            dma((4, CHUNKS)),
            dma((4, CHUNKS)),
            dma,
            dma((2,)),
            dma((chunks, pairs - 1)),
            dma((chunks, pairs - 1)),
            dma((chunks,)),
            dma((chunks,)),
            dma((chunks, pairs)),
            dma((chunks, pairs)),
            dma((chunks, pairs)),
            dma((chunks,)),
            dma((3, 3)),
            dma((3, 3)),
            dma((3, pairs)),
            dma((3, pairs)),
            dma((3, 2 * pairs)),
            dma((3,)),
            dma((2,)),
            dma((pairs,)),
            dma((pairs,)),
            dma((4,)),
            dma((4,)),
        ],
        compiler_params=pltpu.CompilerParams(
            collective_id=2, has_side_effects=True, vmem_limit_bytes=65_500_000
        ),
        name="attention_backward",
    )(span, qkv, out, logsum, factor, weights, small, grad, chip_sum, gathered)


def per_device(
    inputs,
    cotangent,
    gain_attn,
    gain_mlp,
    query_scale,
    w_query,
    w_key,
    w_value,
    w_out,
    w_up,
    w_down,
    lengths,
    offsets,
):
    low = jnp.bfloat16
    f32 = jnp.float32
    here = Place()
    n_dp = lax.axis_size("dp")
    local_rows, model = inputs.shape
    seq_slots = local_rows * 4
    width_local = w_query.shape[1]
    head_dim = query_scale.shape[0]
    heads_local = width_local // head_dim
    pairs = n_dp // 2
    swap_core = [(i, i ^ 1) for i in range(n_dp)]

    split = min(pairs, 4)
    mlp_native = jnp.stack([w_out, jnp.transpose(w_up), w_down])
    mlp_native = mlp_native.reshape(3, split, width_local // split, model)
    native = jnp.concatenate(
        [jnp.transpose(w_query), jnp.transpose(w_key), jnp.transpose(w_value)]
    )
    own_span = jnp.concatenate([lengths, offsets])
    other_span = lax.ppermute(own_span, "dp", swap_core)
    group_span = jnp.where(here.main, own_span, other_span)
    residual = inputs.astype(f32)
    normed, inverse_one = rms_forward(residual, gain_attn)
    scale_const = LOG_TWO_E / math.sqrt(head_dim)
    soft = jax.nn.softplus(query_scale)
    factor = jnp.tile(soft * scale_const, heads_local)[:, None]
    gathered, stacked_w, qkv, attended, logsum, attended_rows, *mlp_w = attention_forward(
        group_span,
        normed.astype(low),
        native,
        jnp.concatenate([factor, jnp.ones((2 * width_local, 1), f32)]),
        mlp_native,
        heads_local,
    )
    w_out_all, w_up_all, w_down_all = (weight.reshape(model, model) for weight in mlp_w)
    output, grad_hidden, chip_sum, small, grad_attended = feed_forward(
        own_span, gain_mlp[None], attended_rows, inputs, cotangent, w_out_all, w_up_all, w_down_all,
        width_local, pairs,
    )
    grad_first, grad_out, grad_up, grad_down, qkv_all, small = attention_backward(
        group_span, qkv, attended, logsum, factor, stacked_w, small, grad_attended, chip_sum, gathered
    )
    grad_input = grad_hidden + rms_backward(
        residual, inverse_one, gain_attn, grad_first.astype(f32)
    )
    grad_gain_one = small[0] / gain_attn
    grad_gain_two = small[1] / gain_mlp
    scale_sum = jnp.sum(small[2, :width_local].reshape(heads_local, head_dim), axis=0)
    grad_scale = scale_sum * jax.nn.sigmoid(query_scale) / soft
    qkv_all = qkv_all.reshape(3 * width_local, model)

    def final(weight):
        return weight.reshape(width_local, model).astype(f32)

    return (
        output,
        grad_input,
        grad_gain_one,
        grad_gain_two,
        grad_scale,
        jnp.transpose(final(qkv_all[:width_local])),
        jnp.transpose(final(qkv_all[width_local:2 * width_local])),
        jnp.transpose(final(qkv_all[2 * width_local:3 * width_local])),
        final(grad_out),
        jnp.transpose(final(grad_up)),
        final(grad_down),
    )


def solution(mesh):
    rows = P(("dp", "tensor"), None)
    cols_t = P(None, "tensor")
    rows_t = P("tensor", None)
    return jax.shard_map(
        per_device,
        mesh=mesh,
        in_specs=(
            rows, rows, P(), P(), P(), cols_t, cols_t, cols_t, rows_t, cols_t, rows_t, P("dp"), P("dp"),
        ),
        out_specs=(
            rows, rows, P(), P(), P(), cols_t, cols_t, cols_t, rows_t, cols_t, rows_t,
        ),
        check_vma=False,
    )
```

profile of v0, /device:TPU:27, one launch (start us, length us, event | category | flops | bytes accessed | tf_op | source)
XLA Modules:
  0.0 327.6 jit_solution(15244313964904057474)
XLA Ops:
  0.6 0.0 copy-start.4
  0.7 0.0 copy-start.11
  0.7 0.0 copy-start.12
  2.2 0.1 pad_add_fusion.span
  2.3 0.7 collective-permute-start
  3.0 0.7 broadcast_multiply_fusion.1
  3.6 1.7 fusion.8
  5.3 1.3 broadcast_in_dim.2.gain
  6.6 0.2 broadcast_in_dim_tile.4.factor
  6.8 0.0 copy-start.9
  6.8 0.0 copy-start.13
  6.8 0.0 copy-done.4
  6.9 2.2 fusion.3.own
  9.1 0.0 copy-done.13
  9.1 0.0 copy-start.14
  9.1 0.0 copy-start.15
  9.1 0.0 copy-start.16
  9.1 1.6 pad_maximum_fusion.native
  10.7 0.5 copy-done.15
  11.2 0.4 copy-done.16
  11.6 1.8 pad_maximum_fusion.1.mlp_native
  13.4 0.0 collective-permute-done
  13.4 0.1 broadcast_select_fusion.span
  13.5 118.5 %attention_forward.1 = (bf16[2048,1280]{1,0:T(8,128)(2,1)}, bf16[960,1280]{1,0:T(8,128)(2,1)}, bf16[960,2048]{1,0:T(8,128)(2,1)}, bf16[320,2048]{1,0:T(8,128)(2,...) custom-call(s32[2]{0:T(128)S(1)} %broadcast_select_fusion.span, ...), custom_call_target="tpu_custom_call" | custom-call | tf_op jit(solution)/shard_map/attention_forward/pallas_call | solution.py:474
  131.9 0.0 copy-start
  131.9 1.0 copy-done
  133.0 1.1 copy-done.1
  134.1 0.6 copy-done.2
  134.7 53.5 %feed_forward.1 = (bf16[512,1280]{1,0:T(8,128)(2,1)}, f32[512,1280]{1,0:T(8,128)}, bf16[3,4,4,80,640]{4,3,2,1,0:T(8,128)(2,1)}, f32[8,1280]{1,0:T(8,128)}, bf16[320,2048]{1,0:T(8,128)(2,1)}) custom-call(s32[2]{0:T(128)} %copy-done.22, f32[1,1280]{1,0:T(1,128)} %broadcast_in_dim.2.gain, bf16[1280,512]{1,0:T(8,128)(2,1)} %copy-done.1, ...), custom_call_target="tpu_custom_call" | custom-call | tf_op jit(solution)/shard_map/feed_forward/pallas_call | solution.py:666
  188.2 0.0 copy-start.5
  188.2 0.0 copy-start.20
  188.2 123.2 %attention_backward.1 = (bf16[512,1280]{1,0:T(8,128)(2,1)}, bf16[4,80,1280]{2,1,0:T(8,128)(2,1)}, bf16[4,80,1280]{2,1,0:T(8,128)(2,1)}, bf16[4,80,1280]{2,1,0:T(...) custom-call(s32[2]{0:T(128)} %copy-done.3, bf16[960,2048]{1,0:T(8,128)(2,1)} %get-tuple-element.37.qkv, ...), custom_call_target="tpu_custom_call" | custom-call | tf_op jit(solution)/shard_map/attention_backward/pallas_call | solution.py:1281
  311.4 0.0 copy-start.21
  311.5 0.0 copy-start.23
  311.5 0.8 slice_reduce_fusion.2
  312.3 0.9 slice_reduce_fusion
  313.2 1.9 fusion.4
  315.2 0.6 div.32
  315.8 0.1 reshape_squeeze.3
  315.9 0.5 fusion.9
  316.4 0.6 div.31
  317.0 1.3 bitcast_convert_fusion.1
  318.4 0.0 copy-done.8
  318.4 2.6 convert_bitcast_fusion.1
  321.0 1.3 copy-done.7
  322.3 2.2 fusion.7
  324.5 2.1 convert_bitcast_fusion
  326.6 1.1 copy.29
  (31 shorter events, 0.1 us)
Async XLA Ops:
  0.6 6.2 %copy-start.4 = (bf16[512,1280]{1,0:T(8,128)(2,1)S(1)}, bf16[512,1280]{1,0:T(8,128)(2,1)}, u32[]{:S(2)}) copy-start(bf16[512,1280]{1,0:T(8,128)(2,1)} %residual.1) | copy-start | bytes 3932164
  0.7 8.4 %copy-start.11 = (bf16[1280,320]{0,1:T(8,128)(2,1)S(1)}, bf16[1280,320]{0,1:T(8,128)(2,1)}, u32[]{:S(2)}) copy-start(bf16[1280,320]{0,1:T(8,128)(2,1)} %param.20) | copy-start | bytes 2457604
  0.7 8.4 %copy-start.12 = (bf16[1280,320]{0,1:T(8,128)(2,1)S(1)}, bf16[1280,320]{0,1:T(8,128)(2,1)}, u32[]{:S(2)}) copy-start(bf16[1280,320]{0,1:T(8,128)(2,1)} %param.19) | copy-start | bytes 2457604
  2.3 8.4 %copy-start.22 = (s32[2]{0:T(128)}, s32[2]{0:T(128)S(1)}, u32[]{:S(2)}) copy-start(s32[2]{0:T(128)S(1)} %pad_add_fusion.span) | copy-start | bytes 28
  2.3 11.1 %collective-permute-start = (s32[2]{0:T(128)S(1)}, s32[2]{0:T(128)S(1)}, u32[]{:S(2)}, u32[]{:S(2)}) collective-permute-start(s32[2]{0:T(128)S(1)} %pad_add_fusion.span), channel_id=1, source_target_pairs={{0,4},{4,0},{8,12},{12,8},{16,20},{20,16},{24,28},{28,24},{1,5},{5... | collective-permute-start | bytes 32 | tf_op jit(solution)/shard_map/ppermute | solution.py:1389
  6.8 4.0 %copy-start.9 = (f32[320,1]{1,0:T(8,128)}, f32[320,1]{1,0:T(8,128)S(1)}, u32[]{:S(2)}) copy-start(f32[320,1]{1,0:T(8,128)S(1)} %broadcast_in_dim_tile.4.factor) | copy-start | bytes 3844
  6.8 2.3 copy-start.13
  9.1 1.6 copy-start.14
  9.1 2.1 copy-start.15
  9.1 2.5 copy-start.16
  13.5 118.5 %copy-start.3 = (s32[2]{0:T(128)}, s32[2]{0:T(128)S(1)}, u32[]{:S(2)}) copy-start(s32[2]{0:T(128)S(1)} %broadcast_select_fusion.span) | copy-start | bytes 28
  131.9 1.1 copy-start
  133.0 1.1 copy-start.1
  134.1 0.6 copy-start.2
  188.2 125.0 %copy-start.5 = (bf16[512,1280]{1,0:T(8,128)(2,1)S(1)}, bf16[512,1280]{1,0:T(8,128)(2,1)}, u32[]{:S(2)}) copy-start(bf16[512,1280]{1,0:T(8,128)(2,1)} %residual.1) | copy-start | bytes 3932164
  188.2 125.0 %copy-start.20 = (f32[1280]{0:T(1024)S(1)}, f32[1280]{0:T(1024)}, u32[]{:S(2)}) copy-start(f32[1280]{0:T(1024)} %param.15) | copy-start | bytes 15364
  311.4 3.7 %copy-start.21 = (f32[1280]{0:T(1024)S(1)}, f32[1280]{0:T(1024)}, u32[]{:S(2)}) copy-start(f32[1280]{0:T(1024)} %param.16) | copy-start | bytes 15364
  311.5 4.4 %copy-start.23 = (f32[80]{0:T(128)S(1)}, f32[80]{0:T(128)}, u32[]{:S(2)}) copy-start(f32[80]{0:T(128)} %param.17) | copy-start | bytes 964
  311.5 5.6 %copy-start.19 = (bf16[4,80,1280]{2,1,0:T(8,128)(2,1)S(1)}, bf16[4,80,1280]{2,1,0:T(8,128)(2,1)}, u32[]{:S(2)}) copy-start(bf16[4,80,1280]{2,1,0:T(8,128)(2,1)} %get-tuple-element.48) | copy-start | bytes 2457604
  315.9 2.5 copy-start.8
  318.4 2.6 copy-start.6
  318.4 3.9 %copy-start.7 = (f32[512,1280]{1,0:T(8,128)S(1)}, f32[512,1280]{1,0:T(8,128)}, u32[]{:S(2)}) copy-start(f32[512,1280]{1,0:T(8,128)} %get-tuple-element.36) | copy-start | bytes 7864324
  322.3 2.2 copy-start.17
  322.3 2.2 copy-start.18
  324.5 2.1 copy-start.10
where the time goes:
time: 330 us; the launch traced here: 328 us
  Pallas kernels  295 us (89%)
  other arithmetic  20 us (6%)
  local copies, waits for them, and re-layouts  9.32 us (3%)
    pallas_call x1, Pallas kernels, attention_backward(): pl.pallas_call(backward_kernel, out_shape=(jax.ShapeDtypeStruct((rows, mo...  123 us
    pallas_call x1, Pallas kernels, attention_forward(): pl.pallas_call(forward_kernel, out_shape=(jax.ShapeDtypeStruct((slots, mo...  118 us
    pallas_call x1, Pallas kernels, feed_forward(): pl.pallas_call(middle_kernel, out_shape=(jax.ShapeDtypeStruct((rows, mode...  53.5 us
  transfers between devices with their start and end apart: 1, of which 0 were waited for; matrix products, arithmetic and copies ran while one was open for 3% of the time, Pallas kernels for 0%

commit v1 on v0

--- a/solution.py
+++ b/solution.py
@@ -11,7 +11,8 @@
 EPSILON = 1e-06
 LOG_TWO_E = 1.4426950408889634
 MESH_ID = pl.DeviceIdType.MESH
-CHUNKS = 4
+CHUNKS = 8
+BACK_CHUNKS = 2
 
 
 def rms_forward(values, gain):
@@ -713,7 +714,7 @@
     here = Place()
     pairs = here.pairs
     rows = rows_grad.shape[0]
-    part = rows // CHUNKS
+    part = rows // BACK_CHUNKS
     partner = here.partner()
     pair_barrier(here, plane=True)
     blocks = slots // TILE
@@ -851,12 +852,12 @@
         return core_sum(k, ch) + from_line[line_piece(k, ch)].astype(f32)
 
     def pass_on(k):
-        for ch in range(CHUNKS):
+        for ch in range(BACK_CHUNKS):
             partial[span_of(here.g, k, ch)] = core_sum(k, ch).astype(low)
             line_copy(k, ch).start()
 
     def send_home(k):
-        for ch in range(CHUNKS):
+        for ch in range(BACK_CHUNKS):
             partial[span_of(here.g, k, ch)] = with_line(k, ch).astype(low)
             home_copy(k, ch).start()
 
@@ -943,7 +944,7 @@
 
         @pl.when(jnp.logical_not(here.main))
         def _():
-            for ch in range(CHUNKS):
+            for ch in range(BACK_CHUNKS):
                 core_copy(k, ch).start()
 
     plane_total(2)
@@ -1171,17 +1172,17 @@
 
     @pl.when(here.pos == 0)
     def _():
-        for ch in range(CHUNKS):
+        for ch in range(BACK_CHUNKS):
             rows_grad[line_rows(ch)] = with_line(0, ch).astype(low)
         for k in (1, 2, 3):
-            for ch in range(CHUNKS):
+            for ch in range(BACK_CHUNKS):
                 line_copy(k, ch).wait_send()
 
     @pl.when(here.pos == 1)
     def _():
-        for ch in range(CHUNKS):
+        for ch in range(BACK_CHUNKS):
             rows_grad[line_rows(ch)] = with_line(1, ch).astype(low)
-        for ch in range(CHUNKS):
+        for ch in range(BACK_CHUNKS):
             line_copy(0, ch).wait_send()
             for k in (2, 3):
                 home_copy(k, ch).wait_send()
@@ -1189,7 +1190,7 @@
     for k in (2, 3):
         @pl.when(here.pos == k)
         def _(k=k):
-            for ch in range(CHUNKS):
+            for ch in range(BACK_CHUNKS):
                 remote(
                     partial.at[piece(0, ch)], rows_grad.at[line_rows(ch)], send_z.at[0, ch], recv_z.at[k, ch], partner
                 ).wait_recv()
@@ -1233,7 +1234,7 @@
                 qkv_core(i, step).wait_recv()
 
         for k in range(4):
-            for ch in range(CHUNKS):
+            for ch in range(BACK_CHUNKS):
                 core_copy(k, ch).wait_send()
 
     for w in range(3):
@@ -1319,10 +1320,10 @@
             dma((2,)),
             dma((3, max(6, pairs - 1))),
             dma((3, max(6, pairs - 1))),
-            dma((4, CHUNKS)),
-            dma((4, CHUNKS)),
-            dma((4, CHUNKS)),
-            dma((4, CHUNKS)),
+            dma((4, BACK_CHUNKS)),
+            dma((4, BACK_CHUNKS)),
+            dma((4, BACK_CHUNKS)),
+            dma((4, BACK_CHUNKS)),
             dma,
             dma((2,)),
             dma((chunks, pairs - 1)),

time: 330 us -> 328 us (level)
    pallas_call x1, Pallas kernels: 53.5 us -> 45 us  [feed_forward(): pl.pallas_call(middle_kernel, out_shape=(jax.ShapeDtypeStruct((rows, mode...]
    pallas_call x1, Pallas kernels: 118 us -> 126 us  [attention_forward(): pl.pallas_call(forward_kernel, out_shape=(jax.ShapeDtypeStruct((slots, mo...]
where the time goes in v1:
time: 328 us; the launch traced here: 325 us
  Pallas kernels  293 us (89%)
  other arithmetic  20 us (6%)
  local copies, waits for them, and re-layouts  9.32 us (3%)
    pallas_call x1, Pallas kernels, attention_forward(): pl.pallas_call(forward_kernel, out_shape=(jax.ShapeDtypeStruct((slots, mo...  126 us
    pallas_call x1, Pallas kernels, attention_backward(): pl.pallas_call(backward_kernel, out_shape=(jax.ShapeDtypeStruct((rows, mo...  122 us
    pallas_call x1, Pallas kernels, feed_forward(): pl.pallas_call(middle_kernel, out_shape=(jax.ShapeDtypeStruct((rows, mode...  45 us
  transfers between devices with their start and end apart: 1, of which 0 were waited for; matrix products, arithmetic and copies ran while one was open for 3% of the time, Pallas kernels for 0%

profile of v1, /device:TPU:27, one launch (start us, length us, event | category | flops | bytes accessed | tf_op | source)
XLA Modules:
  0.0 325.3 jit_solution(8186137153314850159)
XLA Ops:
  0.6 0.0 copy-start.4
  2.2 0.1 pad_add_fusion.span
  2.3 0.7 collective-permute-start
  3.0 0.7 broadcast_multiply_fusion.1
  3.6 1.7 fusion.8
  5.3 1.3 broadcast_in_dim.2.gain
  6.6 0.2 broadcast_in_dim_tile.4.factor
  6.8 0.0 copy-start.9
  6.8 0.0 copy-start.13
  6.8 0.0 copy-done.4
  6.9 2.2 fusion.3.own
  9.1 0.0 copy-done.12
  9.1 0.0 copy-start.14
  9.1 0.0 copy-start.15
  9.1 0.0 copy-start.16
  9.1 1.6 pad_maximum_fusion.native
  10.7 0.0 copy-done.9
  10.7 0.5 copy-done.15
  11.2 0.4 copy-done.16
  11.6 1.8 pad_maximum_fusion.1.mlp_native
  13.4 0.0 collective-permute-done
  13.4 0.1 broadcast_select_fusion.span
  13.5 125.9 %attention_forward.1 = (bf16[2048,1280]{1,0:T(8,128)(2,1)}, bf16[960,1280]{1,0:T(8,128)(2,1)}, bf16[960,2048]{1,0:T(8,128)(2,1)}, bf16[320,2048]{1,0:T(8,128)(2,...) custom-call(s32[2]{0:T(128)S(1)} %broadcast_select_fusion.span, ...), custom_call_target="tpu_custom_call" | custom-call | tf_op jit(solution)/shard_map/attention_forward/pallas_call | solution.py:475
  139.4 0.0 copy-start
  139.4 1.0 copy-done
  140.4 1.1 copy-done.1
  141.5 0.6 copy-done.2
  142.1 45.0 %feed_forward.1 = (bf16[512,1280]{1,0:T(8,128)(2,1)}, f32[512,1280]{1,0:T(8,128)}, bf16[3,4,4,80,640]{4,3,2,1,0:T(8,128)(2,1)}, f32[8,1280]{1,0:T(8,128)}, bf16[320,2048]{1,0:T(8,128)(2,1)}) custom-call(s32[2]{0:T(128)} %copy-done.22, f32[1,1280]{1,0:T(1,128)} %broadcast_in_dim.2.gain, bf16[1280,512]{1,0:T(8,128)(2,1)} %copy-done.1, ...), custom_call_target="tpu_custom_call" | custom-call | tf_op jit(solution)/shard_map/feed_forward/pallas_call | solution.py:667
  187.1 0.0 copy-start.5
  187.1 0.0 copy-start.20
  187.1 122.1 %attention_backward.1 = (bf16[512,1280]{1,0:T(8,128)(2,1)}, bf16[4,80,1280]{2,1,0:T(8,128)(2,1)}, bf16[4,80,1280]{2,1,0:T(8,128)(2,1)}, bf16[4,80,1280]{2,1,0:T(...) custom-call(s32[2]{0:T(128)} %copy-done.3, bf16[960,2048]{1,0:T(8,128)(2,1)} %get-tuple-element.37.qkv, ...), custom_call_target="tpu_custom_call" | custom-call | tf_op jit(solution)/shard_map/attention_backward/pallas_call | solution.py:1282
  309.2 0.0 copy-start.21
  309.2 0.0 copy-start.23
  309.2 0.0 copy-start.19
  309.2 0.8 slice_reduce_fusion.2
  310.0 0.9 slice_reduce_fusion
  310.9 0.0 copy-done.5
  310.9 1.9 fusion.4
  312.9 0.6 div.32
  313.5 0.1 reshape_squeeze.3
  313.6 0.5 fusion.9
  314.1 0.6 div.31
  314.7 1.3 bitcast_convert_fusion.1
  316.1 2.6 convert_bitcast_fusion.1
  318.7 1.3 copy-done.7
  320.0 2.2 fusion.7
  322.2 2.1 convert_bitcast_fusion
  324.3 1.1 copy.29
  (31 shorter events, 0.1 us)
Async XLA Ops:
  0.6 6.2 %copy-start.4 = (bf16[512,1280]{1,0:T(8,128)(2,1)S(1)}, bf16[512,1280]{1,0:T(8,128)(2,1)}, u32[]{:S(2)}) copy-start(bf16[512,1280]{1,0:T(8,128)(2,1)} %residual.1) | copy-start | bytes 3932164
  0.7 8.4 %copy-start.11 = (bf16[1280,320]{0,1:T(8,128)(2,1)S(1)}, bf16[1280,320]{0,1:T(8,128)(2,1)}, u32[]{:S(2)}) copy-start(bf16[1280,320]{0,1:T(8,128)(2,1)} %param.20) | copy-start | bytes 2457604
  0.7 8.4 %copy-start.12 = (bf16[1280,320]{0,1:T(8,128)(2,1)S(1)}, bf16[1280,320]{0,1:T(8,128)(2,1)}, u32[]{:S(2)}) copy-start(bf16[1280,320]{0,1:T(8,128)(2,1)} %param.19) | copy-start | bytes 2457604
  2.3 8.4 %copy-start.22 = (s32[2]{0:T(128)}, s32[2]{0:T(128)S(1)}, u32[]{:S(2)}) copy-start(s32[2]{0:T(128)S(1)} %pad_add_fusion.span) | copy-start | bytes 28
  2.3 11.1 %collective-permute-start = (s32[2]{0:T(128)S(1)}, s32[2]{0:T(128)S(1)}, u32[]{:S(2)}, u32[]{:S(2)}) collective-permute-start(s32[2]{0:T(128)S(1)} %pad_add_fusion.span), channel_id=1, source_target_pairs={{0,4},{4,0},{8,12},{12,8},{16,20},{20,16},{24,28},{28,24},{1,5},{5... | collective-permute-start | bytes 32 | tf_op jit(solution)/shard_map/ppermute | solution.py:1390
  6.8 4.0 %copy-start.9 = (f32[320,1]{1,0:T(8,128)}, f32[320,1]{1,0:T(8,128)S(1)}, u32[]{:S(2)}) copy-start(f32[320,1]{1,0:T(8,128)S(1)} %broadcast_in_dim_tile.4.factor) | copy-start | bytes 3844
  6.8 2.3 copy-start.13
  9.1 1.6 copy-start.14
  9.1 2.1 copy-start.15
  9.1 2.5 copy-start.16
  13.5 125.9 %copy-start.3 = (s32[2]{0:T(128)}, s32[2]{0:T(128)S(1)}, u32[]{:S(2)}) copy-start(s32[2]{0:T(128)S(1)} %broadcast_select_fusion.span) | copy-start | bytes 28
  139.4 1.1 copy-start
  140.4 1.1 copy-start.1
  141.5 0.6 copy-start.2
  187.1 123.8 %copy-start.5 = (bf16[512,1280]{1,0:T(8,128)(2,1)S(1)}, bf16[512,1280]{1,0:T(8,128)(2,1)}, u32[]{:S(2)}) copy-start(bf16[512,1280]{1,0:T(8,128)(2,1)} %residual.1) | copy-start | bytes 3932164
  187.1 123.8 %copy-start.20 = (f32[1280]{0:T(1024)S(1)}, f32[1280]{0:T(1024)}, u32[]{:S(2)}) copy-start(f32[1280]{0:T(1024)} %param.15) | copy-start | bytes 15364
  309.2 3.7 %copy-start.21 = (f32[1280]{0:T(1024)S(1)}, f32[1280]{0:T(1024)}, u32[]{:S(2)}) copy-start(f32[1280]{0:T(1024)} %param.16) | copy-start | bytes 15364
  309.2 4.4 %copy-start.23 = (f32[80]{0:T(128)S(1)}, f32[80]{0:T(128)}, u32[]{:S(2)}) copy-start(f32[80]{0:T(128)} %param.17) | copy-start | bytes 964
  309.2 5.6 %copy-start.19 = (bf16[4,80,1280]{2,1,0:T(8,128)(2,1)S(1)}, bf16[4,80,1280]{2,1,0:T(8,128)(2,1)}, u32[]{:S(2)}) copy-start(bf16[4,80,1280]{2,1,0:T(8,128)(2,1)} %get-tuple-element.48) | copy-start | bytes 2457604
  313.6 2.5 copy-start.8
  316.1 2.6 copy-start.6
  316.1 3.9 %copy-start.7 = (f32[512,1280]{1,0:T(8,128)S(1)}, f32[512,1280]{1,0:T(8,128)}, u32[]{:S(2)}) copy-start(f32[512,1280]{1,0:T(8,128)} %get-tuple-element.36) | copy-start | bytes 7864324
  320.0 2.2 copy-start.17
  320.0 2.2 copy-start.18
  322.2 2.1 copy-start.10
